TPU v7x, 32 devices: a whole 2x2x4 slice. The times are simulated.
32 devices in a mesh: grp: 2 (over y), chan: 2 (over x), tm: 4 (over z), pol: 2 (over core).
Axes of the slice: x: 2, y: 2, z: 4, core: 2. Of those that a mesh axis runs over, the one named last changes fastest.
Arguments:
- voltages: bfloat16 [4, 2, 256, 32768], P('grp', 'pol', 'chan', 'tm'), parts along dimension 0, may hold values from -6 to 6
- taps_filter: float32 [16, 2048], replicated, may hold values from -1.5 to 1.5
- tile_a: int32 [14, 64], replicated, may hold values from 0 to 255
- tile_b: int32 [14, 64], replicated, may hold values from 0 to 255
- tile_owner: int32 [14], replicated, may hold values from 0 to 1, as said below
- tile_flags: int32 [14, 16], replicated, may hold values 0 or 1
Outputs:
- visibility: float32 [16, 256, 4, 2, 64, 128], P('pol', ('chan', 'tm'), 'grp'), parts along dimension 2
There are 2 independent parts, one for each index of `grp`. A program takes and returns all parts, laid end to end along the dimension named above; an argument that names none is the same for every part. Nothing has to cross between parts.
Inputs may be any that keep to these rules, and one draw needn't show every extreme that they name: `tile_owner`: one owner holds exactly 8 tiles and the other owner holds all the rest.
All inputs are finite; a program needn't handle non-finite values.
Results may differ from a plain program's by a relative error of at most 0.0035.
Values may be sent and summed in bfloat16 or wider, within the bound.
A program may use at most 128 MiB of HBM per device.

v0:
```python
import math
import jax
import jax.numpy as jnp
from jax import lax
from jax.sharding import PartitionSpec as P

AVG = 8
CAP = 8
radix_first = 32


def from_behind(value, axis, steps):
    count = lax.axis_size(axis)
    first, last = (max(0, -steps), min(count, count - steps))
    return lax.ppermute(value, axis, [(source, source + steps) for source in range(first, last)])


def fourier(filtered):
    length = filtered.shape[-1]
    second = length // radix_first
    exact_mode = lax.Precision.HIGHEST
    grid = filtered.reshape(filtered.shape[:-1] + (radix_first, second))
    outer = jnp.arange(radix_first, dtype=jnp.int32)
    inner = jnp.arange(second, dtype=jnp.int32)
    phase_one = (
        2.0
        * math.pi
        / radix_first
        * (outer[:, None] * outer[None, :] % radix_first).astype(jnp.float32)
    )
    phase_twist = 2.0 * math.pi / length * (outer[:, None] * inner[None, :]).astype(jnp.float32)
    phase_two = (
        2.0 * math.pi / second * (inner[:, None] * inner[None, :] % second).astype(jnp.float32)
    )
    cos_one, sin_one = (jnp.cos(phase_one), jnp.sin(phase_one))
    cos_twist, sin_twist = (jnp.cos(phase_twist), jnp.sin(phase_twist))
    cos_two, sin_two = (jnp.cos(phase_two), jnp.sin(phase_two))
    first_form = "fk,stkj->stfj"
    section_re = jnp.einsum(first_form, cos_one, grid[0], precision=exact_mode) + jnp.einsum(
        first_form, sin_one, grid[1], precision=exact_mode
    )
    section_im = jnp.einsum(first_form, cos_one, grid[1], precision=exact_mode) - jnp.einsum(
        first_form, sin_one, grid[0], precision=exact_mode
    )
    turned_re = section_re * cos_twist + section_im * sin_twist
    turned_im = section_im * cos_twist - section_re * sin_twist
    second_form = "gj,stfj->stgf"
    final_re = jnp.einsum(second_form, cos_two, turned_re, precision=exact_mode) + jnp.einsum(
        second_form, sin_two, turned_im, precision=exact_mode
    )
    final_im = jnp.einsum(second_form, cos_two, turned_im, precision=exact_mode) - jnp.einsum(
        second_form, sin_two, turned_re, precision=exact_mode
    )
    joined = jnp.stack([final_re, final_im]).reshape(filtered.shape)
    return joined * (1.0 / math.sqrt(length))


def correlate(full, rows_a, rows_b, flags, group_count):
    depth = full.shape[4]
    weight = jnp.tile(flags.astype(jnp.bfloat16), depth // flags.shape[0])
    left_rows = jnp.take(full, rows_a, axis=2) * weight
    right_rows = jnp.take(full, rows_b, axis=2)
    stacked_left = jnp.stack(
        [
            jnp.concatenate([left_rows[0], left_rows[1]], axis=-1),
            jnp.concatenate([left_rows[1], -left_rows[0]], axis=-1),
        ]
    )
    joined_right = jnp.concatenate([right_rows[0], right_rows[1]], axis=-1)
    result = jnp.einsum(
        "rpank,qbnk->nrpaqb", stacked_left, joined_right, preferred_element_type=jnp.float32
    )
    width = rows_a.shape[0]
    return result.reshape(group_count, 2, 2, width, 2 * width) * (1.0 / depth)


def on_device(voltages, taps_filter, tile_a, tile_b, tile_owner, tile_flags):
    history = taps_filter.shape[0] - 1
    length = taps_filter.shape[1]
    stations = voltages.shape[2]
    frames = voltages.shape[3] // length
    local_blocks = voltages.reshape(2, stations, frames, length)
    hop_count = -(-history // frames)
    sending = local_blocks
    extended = local_blocks
    for hop_index in range(hop_count):
        sending = from_behind(sending, "tm", 1)
        extended = jnp.concatenate([sending, extended], axis=2)
    extended = extended[:, :, extended.shape[2] - history - frames :]
    filtered = jnp.zeros((2, stations, frames, length), jnp.float32)
    for tap_index in range(history + 1):
        start = history - tap_index
        filtered = filtered + taps_filter[tap_index] * extended[
            :, :, start : start + frames
        ].astype(jnp.float32)
    spectra = fourier(filtered).astype(jnp.bfloat16)
    chan_count = lax.axis_size("chan")
    time_count = lax.axis_size("tm")
    narrow = length // (chan_count * time_count)
    outgoing = spectra.reshape(2, stations, frames, chan_count, time_count, narrow)
    outgoing = outgoing.transpose(0, 3, 4, 5, 1, 2)
    flat = outgoing.reshape(2, chan_count * time_count, narrow, stations * frames)
    moved = lax.all_to_all(flat, ("chan", "tm"), split_axis=1, concat_axis=1, tiled=True)
    moved = moved.reshape(2, chan_count, time_count, narrow, stations, frames)
    bands = narrow // AVG
    every_station = chan_count * stations
    spectra_count = time_count * frames
    arranged = moved.transpose(0, 1, 4, 3, 2, 5).reshape(
        2, 1, every_station, bands, AVG * spectra_count
    )
    full = lax.all_gather(arranged, "pol", axis=1, tiled=True)
    position = lax.axis_index("pol")
    width = tile_a.shape[1]
    capacity = CAP
    held = tile_owner == position
    listed = jnp.nonzero(held, size=capacity, fill_value=0)[0].astype(jnp.int32)
    tally = jnp.sum(held.astype(jnp.int32))
    initial = jnp.zeros((capacity, bands, 2, 2, width, 2 * width), jnp.float32)

    def fill_slot(slot, results):
        chosen_tile = listed[slot]
        return results.at[slot].set(
            correlate(
                full, tile_a[chosen_tile], tile_b[chosen_tile], tile_flags[chosen_tile], bands
            )
        )

    visibility = lax.fori_loop(0, tally, fill_slot, initial)
    return visibility


def solution(mesh):
    return jax.shard_map(
        on_device,
        mesh=mesh,
        in_specs=(P("grp", "pol", "chan", "tm"), P(), P(), P(), P(), P()),
        out_specs=P("pol", ("chan", "tm"), "grp", None, None, None),
        check_vma=False,
    )
```

profile of v0, /device:TPU:0, one launch (start us, length us, event | category | flops | bytes accessed | tf_op | source)
XLA Modules:
  0.0 1050.4 jit_solution(11831721690737286427)
XLA Ops:
  18.1 89.9 %collective-permute-done = bf16[2,128,4,2048]{1,3,2,0:T(8,128)(2,1)S(1)} collective-permute-done((bf16[2,128,4,2048]{1,3,2,0:T(8,128)(2,1)}, bf16[2,128,4,2048]{1,3,2,0:T(8,128)(2,1)S(1)}, u32[]{:S(2)}, u32[]{:S(2)}) %collective-permute-start) | collective-permute-done | bytes 4194336 | tf_op jit(solution)/shard_map/ppermute | solution.py:15
  112.5 88.7 %collective-permute-done.1 = bf16[2,128,4,2048]{1,3,2,0:T(8,128)(2,1)S(1)} collective-permute-done((bf16[2,128,4,2048]{1,3,2,0:T(8,128)(2,1)S(1)}, bf16[2,128,4,2048]{1,3,2,0:T(8,128)(2,1)S(1)}, u32[]{:S(2)}, u32[]{:S(2)}) %collective-permute-start.1) | collective-permute-done | bytes 4194336 | tf_op jit(solution)/shard_map/ppermute | solution.py:15
  205.8 87.8 %collective-permute-done.2 = bf16[2,128,4,2048]{1,3,2,0:T(8,128)(2,1)S(1)} collective-permute-done((bf16[2,128,4,2048]{1,3,2,0:T(8,128)(2,1)S(1)}, bf16[2,128,4,2048]{1,3,2,0:T(8,128)(2,1)S(1)}, u32[]{:S(2)}, u32[]{:S(2)}) %collective-permute-start.2) | collective-permute-done | bytes 4194336 | tf_op jit(solution)/shard_map/ppermute | solution.py:15
  298.5 86.6 %collective-permute-done.3 = bf16[2,128,4,2048]{1,3,2,0:T(8,128)(2,1)S(1)} collective-permute-done((bf16[2,128,4,2048]{1,3,2,0:T(8,128)(2,1)S(1)}, bf16[2,128,4,2048]{1,3,2,0:T(8,128)(2,1)S(1)}, u32[]{:S(2)}, u32[]{:S(2)}) %collective-permute-start.3) | collective-permute-done | bytes 4194336 | tf_op jit(solution)/shard_map/ppermute | solution.py:15
  402.7 24.3 %multiply_add_fusion = f32[2,128,4,2048]{1,3,2,0:T(8,128)} fusion(bf16[2,128,4,2048]{1,3,2,0:T(8,128)(2,1)} %copy-done.4, bf16[2,128,4,2048]{1,3,2,0:T(8,128)(2,1)S(1)} %collective-permute-done.1, bf16[2,128,4,2048]{1,3,2,0:T(8,128)(2,1)} %copy-done.5, bf16[2,128,4,2048]{1,3,2,0:T(8,128)(2,1)} %bitcast.161, bf16[2,128,8,2048]{1,3,2,0:T(8,128)(2,1)} %copy-done.2, ...), kind=kLoop, calls=%fused_computation.44 | loop fusion | flops 104857600 | bytes 63045632 | tf_op jit(solution)/shard_map/add | solution.py:93
  450.9 8.5 fusion.16
  494.1 11.2 %copy.62 = bf16[2,2,4,256,128,4]{3,0,5,4,2,1:T(2,128)(2,1)} copy(bf16[2,2,4,256,128,4]{4,3,2,1,5,0:T(8,128)(2,1)} %fusion.13) | data formatting | bytes 8388608 | tf_op jit(solution)/shard_map/transpose | solution.py:101
  505.4 97.2 %all_to_all.5 = bf16[2,8,256,512]{2,0,3,1:T(2,128)(2,1)} all-to-all(bf16[2,8,256,512]{2,0,3,1:T(2,128)(2,1)} %bitcast.158), channel_id=1, replica_groups=mesh['grp'=2,'chan'=2,'tm'=4,'pol'=2] {'chan','tm'}, dimensions={1} | all-to-all | bytes 8388608 | tf_op jit(solution)/shard_map/all_to_all | solution.py:103
  602.6 19.8 %copy.63 = bf16[2,2,128,256,4,4]{2,1,5,4,3,0:T(2,128)(2,1)} copy(bf16[2,2,128,256,4,4]{3,0,5,2,4,1:T(2,128)(2,1)} %bitcast.159) | data formatting | bytes 8388608 | tf_op jit(solution)/shard_map/transpose | solution.py:108
  630.0 7.8 copy.64
  641.1 14.2 %all-gather.2.cloned.1.call-done = bf16[2,2,256,32,128]{4,3,2,0,1:T(8,128)(2,1)} async-done(((bf16[2,1,256,32,128]{4,3,2,0,1:T(8,128)(2,1)}), bf16[2,2,256,32,128]{4,3,2,0,1:T(8,128)(2,1)}) %all-gather.2.cloned.1.call-update) | async-done | bytes 8388624 | tf_op jit(solution)/shard_map/all_gather | solution.py:111
  655.3 8.4 copy.65
  663.7 11.5 %broadcast_in_dim.13 = f32[8,32,2,2,64,128]{5,4,3,2,1,0:T(8,128)} broadcast(f32[]{:T(128)} %constant.110.clone.1), dimensions={} | broadcast | bytes 33554436 | tf_op jit(solution)/shard_map/broadcast_in_dim | solution.py:118
  675.2 368.1 %while.11 = (s32[]{:T(128)}, f32[8,32,2,2,64,128]{5,4,3,2,1,0:T(8,128)}, s32[]{:T(128)}, s32[8]{0:T(128)S(1)}, s32[14,64]{1,0:T(8,128)}, /*index=5*/bf16[2,2,256...) while((s32[]{:T(128)}, ...), condition=%wide.region_6.8_spmd, body=%wide.region_4.7_spmd.sunk | while | flops 563612416 | bytes 78656224 | solution.py:128
  704.8 8.8 mul.774
  742.9 7.8 copy.109
  750.7 8.8 mul.774
  788.8 7.8 copy.109
  796.6 8.8 mul.774
  842.5 8.8 mul.774
  888.5 8.8 mul.774
  934.4 8.8 mul.774
  980.3 8.8 mul.774
  1026.3 8.8 mul.774
  (223 shorter events, 371.4 us)
Async XLA Ops:
  6.5 291.8 %copy-start.6 = (f32[16,2048]{1,0:T(8,128)S(1)}, f32[16,2048]{1,0:T(8,128)}, u32[]{:S(2)}) copy-start(f32[16,2048]{1,0:T(8,128)} %param.13) | copy-start | bytes 393220
  6.5 648.8 %all-gather.2.cloned.1.call-start = ((), (), s32[]{:S(2)}) async-start(), calls=%async_computation.1 | async-start | bytes 12582912 | tf_op jit(solution)/shard_map/all_gather | solution.py:111
  12.9 95.1 %collective-permute-start = (bf16[2,128,4,2048]{1,3,2,0:T(8,128)(2,1)}, bf16[2,128,4,2048]{1,3,2,0:T(8,128)(2,1)S(1)}, u32[]{:S(2)}, u32[]{:S(2)}) collective-permute-start(bf16[2,128,4,2048]{1,3,2,0:T(8,128)(2,1)} %bitcast.160), channel_id=1, source_target_pairs={{0,2},{2,4},{4,6},{1,3},{3,5},{5,7},{8,10},{10,12},{12,14},{9,11},... | collective-permute-start | bytes 12582920 | tf_op jit(solution)/shard_map/ppermute | solution.py:15
  108.0 185.6 %copy-start.5 = (bf16[2,128,4,2048]{1,3,2,0:T(8,128)(2,1)}, bf16[2,128,4,2048]{1,3,2,0:T(8,128)(2,1)S(1)}, u32[]{:S(2)}) copy-start(bf16[2,128,4,2048]{1,3,2,0:T(8,128)(2,1)S(1)} %collective-permute-done) | copy-start | bytes 12582916
  108.0 93.2 %collective-permute-start.1 = (bf16[2,128,4,2048]{1,3,2,0:T(8,128)(2,1)S(1)}, bf16[2,128,4,2048]{1,3,2,0:T(8,128)(2,1)S(1)}, u32[]{:S(2)}, u32[]{:S(2)}) collective-permute-start(bf16[2,128,4,2048]{1,3,2,0:T(8,128)(2,1)S(1)} %collective-permute-done), channel_id=1, source_target_pairs={{0,2},{2,4},{4,6},{1,3},{3,5},{5,7},{8,10},{10,12},{12,14},{9,11},... | collective-permute-start | bytes 12582920 | tf_op jit(solution)/shard_map/ppermute | solution.py:15
  201.2 92.4 %collective-permute-start.2 = (bf16[2,128,4,2048]{1,3,2,0:T(8,128)(2,1)S(1)}, bf16[2,128,4,2048]{1,3,2,0:T(8,128)(2,1)S(1)}, u32[]{:S(2)}, u32[]{:S(2)}) collective-permute-start(bf16[2,128,4,2048]{1,3,2,0:T(8,128)(2,1)S(1)} %collective-permute-done.1), channel_id=1, source_target_pairs={{0,2},{2,4},{4,6},{1,3},{3,5},{5,7},{8,10},{10,12},{12,14},{9,11},... | collective-permute-start | bytes 12582920 | tf_op jit(solution)/shard_map/ppermute | solution.py:15
  293.6 4.9 copy-start.4
  293.6 91.5 %collective-permute-start.3 = (bf16[2,128,4,2048]{1,3,2,0:T(8,128)(2,1)S(1)}, bf16[2,128,4,2048]{1,3,2,0:T(8,128)(2,1)S(1)}, u32[]{:S(2)}, u32[]{:S(2)}) collective-permute-start(bf16[2,128,4,2048]{1,3,2,0:T(8,128)(2,1)S(1)} %collective-permute-done.2), channel_id=1, source_target_pairs={{0,2},{2,4},{4,6},{1,3},{3,5},{5,7},{8,10},{10,12},{12,14},{9,11},... | collective-permute-start | bytes 12582920 | tf_op jit(solution)/shard_map/ppermute | solution.py:15
  388.9 3.4 copy-start.2
  393.6 5.8 copy-start
  399.4 3.2 copy-start.1
  637.8 0.7 copy-start.7
  663.7 11.5 %copy-start.8 = (s32[6]{0:T(128)S(1)}, s32[6]{0:T(128)}, u32[]{:S(2)}) copy-start(s32[6]{0:T(128)} %constant.105.clone.1) | copy-start | bytes 76
  694.3 1.2 copy-start.3
  740.2 1.2 copy-start.3
  786.1 1.2 copy-start.3
  832.0 1.2 copy-start.3
  878.0 1.2 copy-start.3
  923.9 1.2 copy-start.3
  969.8 1.2 copy-start.3
  1015.8 1.2 copy-start.3
Sparse Core Ops, SparseCore 0:
  637.9 17.3 all-gather.1
where the time goes:
time: 1060 us; the launch traced here: 1050 us
  waiting for transfers between devices  367 us (35%)
  local copies, waits for them, and re-layouts  324 us (31%)
  other arithmetic  139 us (13%)
  blocking collectives  97.2 us (9%)
  matrix products  67.4 us (6%)
  loops' own time  23 us (2%)
  starting transfers between devices  19 us (2%)
  between operations  13.9 us (1%)
    ppermute x4, waiting for transfers between devices, from_behind(): lax.ppermute(value, axis, [(source, source + steps) for source in range(f...  353 us
    mul x16, local copies, waits for them, and re-layouts, correlate(): return result.reshape(group_count, 2, 2, width, 2 * width) * (1.0 / depth)  133 us
    all_to_all x1, blocking collectives, on_device(): lax.all_to_all(flat, ('chan', 'tm'), split_axis=1, concat_axis=1, tiled=T...  97.2 us
    scatter x8, other arithmetic, fill_slot(): results.at[slot]  60.2 us
    gather x8, local copies, waits for them, and re-layouts, correlate(): right_rows = jnp.take(full, rows_b, axis=2)  34.7 us
    gather x8, local copies, waits for them, and re-layouts, correlate(): left_rows = jnp.take(full, rows_a, axis=2) * weight  34.6 us
    add x1, other arithmetic, on_device(): filtered + taps_filter[tap_index] * extended[:, :, start:start + frames]....  24.3 us
    another operation x1, loops' own time, on_device(): visibility = lax.fori_loop(0, tally, fill_slot, initial)  23 us
  transfers between devices with their start and end apart: 5, of which 5 were waited for; matrix products, arithmetic and copies ran while one was open for 0% of the time, Pallas kernels for 0%

commit v1 on v0

--- a/solution.py
+++ b/solution.py
@@ -1,3 +1,4 @@
+import functools
 import math
 import jax
 import jax.numpy as jnp
@@ -7,6 +8,38 @@
 AVG = 8
 CAP = 8
 radix_first = 32
+
+
+def launch_windows(xx, pos_dim, t0):
+    e_next = xx.shape
+    before = xx.reshape(*e_next[:pos_dim], t0, e_next[pos_dim] // t0, *e_next[pos_dim + 1 :])
+    return jnp.moveaxis(before, pos_dim, 0)
+
+
+def wall_try_all(mine, on_dim):
+    b_next = list(mine.shape[1:])
+    b_next[on_dim] *= mine.shape[0]
+    return jnp.moveaxis(mine, 0, on_dim).reshape(b_next)
+
+
+def _mark_tracks(vals, comm_axis, patch, tile_in):
+    z2 = lax.axis_size(comm_axis)
+    part_next = lax.axis_index(comm_axis)
+    finding, long_array = (z2, part_next)
+    a_now = launch_windows(vals, patch, finding)
+    left_arr = a_now
+    dev_j = 1
+    while dev_j < finding:
+        local_out, parts_out = ((long_array + dev_j) % finding, (long_array - dev_j) % finding)
+        field_out = lax.dynamic_index_in_dim(a_now, local_out, 0)
+        raw_out = tuple(((dev_i, (dev_i + dev_j) % finding) for dev_i in range(finding)))
+        arr_now = lax.ppermute(field_out, comm_axis, raw_out)
+        left_arr = lax.dynamic_update_slice_in_dim(left_arr, arr_now, parts_out, axis=0)
+        dev_j = dev_j + 1
+    return wall_try_all(left_arr, tile_in)
+
+
+_show_rails = functools.partial(_mark_tracks, comm_axis=("chan", "tm"), patch=1, tile_in=1)
 
 
 def from_behind(value, axis, steps):
@@ -100,7 +133,7 @@
     outgoing = spectra.reshape(2, stations, frames, chan_count, time_count, narrow)
     outgoing = outgoing.transpose(0, 3, 4, 5, 1, 2)
     flat = outgoing.reshape(2, chan_count * time_count, narrow, stations * frames)
-    moved = lax.all_to_all(flat, ("chan", "tm"), split_axis=1, concat_axis=1, tiled=True)
+    moved = _show_rails(flat)
     moved = moved.reshape(2, chan_count, time_count, narrow, stations, frames)
     bands = narrow // AVG
     every_station = chan_count * stations

time: 1060 us -> 1070 us (level)
  blocking collectives: 97.2 us -> 0 us
  starting transfers between devices: 19 us -> 82.5 us
  local copies, waits for them, and re-layouts: 324 us -> 346 us
  waiting for transfers between devices: 367 us -> 387 us
    all_to_all x1 -> x0, blocking collectives: 97.2 us -> none  [on_device(): lax.all_to_all(flat, ('chan', 'tm'), split_axis=1, concat_axis=1, tiled=T...]
    ppermute x0 -> x7, starting transfers between devices: none -> 59.9 us  [_mark_tracks(): arr_now = lax.ppermute(field_out, comm_axis, raw_out)]
    ppermute x0 -> x7, waiting for transfers between devices: none -> 13.6 us  [_mark_tracks(): arr_now = lax.ppermute(field_out, comm_axis, raw_out)]
    dynamic_update_slice x0 -> x7, local copies, waits for them, and re-layouts: none -> 13.3 us  [_mark_tracks(): lax.dynamic_update_slice_in_dim(left_arr, arr_now, parts_out, axis=0)]
    unnamed x20 -> x22, local copies, waits for them, and re-layouts: 18.8 us -> 23.1 us
  transfers between devices with their start and end apart: 5 -> 12, of which waited for: 5 -> 8; matrix products, arithmetic and copies ran while one was open for 0% -> 1% of each run, Pallas kernels for 0% -> 0%
where the time goes in v1:
time: 1070 us; the launch traced here: 1060 us
  waiting for transfers between devices  387 us (36%)
  local copies, waits for them, and re-layouts  346 us (32%)
  other arithmetic  138 us (13%)
  starting transfers between devices  82.5 us (8%)
  matrix products  67.4 us (6%)
  loops' own time  22.1 us (2%)
  between operations  13.9 us (1%)
    ppermute x4, waiting for transfers between devices, from_behind(): lax.ppermute(value, axis, [(source, source + steps) for source in range(f...  350 us
    mul x16, local copies, waits for them, and re-layouts, correlate(): return result.reshape(group_count, 2, 2, width, 2 * width) * (1.0 / depth)  132 us
    scatter x8, other arithmetic, fill_slot(): results.at[slot]  60.2 us
    ppermute x7, starting transfers between devices, _mark_tracks(): arr_now = lax.ppermute(field_out, comm_axis, raw_out)  59.9 us
    gather x8, local copies, waits for them, and re-layouts, correlate(): right_rows = jnp.take(full, rows_b, axis=2)  34.7 us
    gather x8, local copies, waits for them, and re-layouts, correlate(): left_rows = jnp.take(full, rows_a, axis=2) * weight  34.6 us
    add x1, other arithmetic, on_device(): filtered + taps_filter[tap_index] * extended[:, :, start:start + frames]....  24.4 us
    all_gather x1, waiting for transfers between devices, on_device(): full = lax.all_gather(arranged, 'pol', axis=1, tiled=True)  23.7 us
  transfers between devices with their start and end apart: 12, of which 8 were waited for; matrix products, arithmetic and copies ran while one was open for 1% of the time, Pallas kernels for 0%

profile of v1, /device:TPU:0, one launch (start us, length us, event | category | flops | bytes accessed | tf_op | source)
XLA Modules:
  0.0 1057.3 jit_solution(4682618853087829630)
XLA Ops:
  18.1 89.9 %collective-permute-done = bf16[2,128,4,2048]{1,3,2,0:T(8,128)(2,1)S(1)} collective-permute-done((bf16[2,128,4,2048]{1,3,2,0:T(8,128)(2,1)}, bf16[2,128,4,2048]{1,3,2,0:T(8,128)(2,1)S(1)}, u32[]{:S(2)}, u32[]{:S(2)}) %collective-permute-start) | collective-permute-done | bytes 4194336 | tf_op jit(solution)/shard_map/ppermute | solution.py:48
  112.5 88.7 %collective-permute-done.1 = bf16[2,128,4,2048]{1,3,2,0:T(8,128)(2,1)S(1)} collective-permute-done((bf16[2,128,4,2048]{1,3,2,0:T(8,128)(2,1)S(1)}, bf16[2,128,4,2048]{1,3,2,0:T(8,128)(2,1)S(1)}, u32[]{:S(2)}, u32[]{:S(2)}) %collective-permute-start.1) | collective-permute-done | bytes 4194336 | tf_op jit(solution)/shard_map/ppermute | solution.py:48
  209.6 86.0 %collective-permute-done.2 = bf16[2,128,4,2048]{1,3,2,0:T(8,128)(2,1)} collective-permute-done((bf16[2,128,4,2048]{1,3,2,0:T(8,128)(2,1)S(1)}, bf16[2,128,4,2048]{1,3,2,0:T(8,128)(2,1)}, u32[]{:S(2)}, u32[]{:S(2)}) %collective-permute-start.2) | collective-permute-done | bytes 4194336 | tf_op jit(solution)/shard_map/ppermute | solution.py:48
  302.3 85.2 %collective-permute-done.3 = bf16[2,128,4,2048]{1,3,2,0:T(8,128)(2,1)} collective-permute-done((bf16[2,128,4,2048]{1,3,2,0:T(8,128)(2,1)}, bf16[2,128,4,2048]{1,3,2,0:T(8,128)(2,1)}, u32[]{:S(2)}, u32[]{:S(2)}) %collective-permute-start.3) | collective-permute-done | bytes 4194336 | tf_op jit(solution)/shard_map/ppermute | solution.py:48
  407.4 24.4 %multiply_add_fusion = f32[2,128,4,2048]{1,3,2,0:T(8,128)} fusion(bf16[2,128,4,2048]{1,3,2,0:T(8,128)(2,1)} %collective-permute-done.2, bf16[2,128,4,2048]{1,3,2,0:T(8,128)(2,1)S(1)} %copy-done.5, bf16[2,128,4,2048]{1,3,2,0:T(8,128)(2,1)} %copy-done.6, bf16[2,128,4,2048]{1,3,2,0:T(8,128)(2,1)} %bitcast.180, bf16[2,128,8,2048]{1,3,2,0:T(8,128)(2,1)} %copy-done.2, ...), kind=kLoop, calls=%fused_computation.44 | loop fusion | flops 104857600 | bytes 63045632 | tf_op jit(solution)/shard_map/add | solution.py:126
  455.8 8.5 fusion.16
  498.9 11.2 %copy.62 = bf16[2,2,4,256,128,4]{3,0,5,4,2,1:T(2,128)(2,1)} copy(bf16[2,2,4,256,128,4]{4,3,2,1,5,0:T(8,128)(2,1)} %fusion.13) | data formatting | bytes 8388608 | tf_op jit(solution)/shard_map/transpose | solution.py:134
  524.5 9.0 collective-permute-done.4
  533.6 23.4 %collective-permute-start.9 = (bf16[1,2,1,256,512]{3,1,4,0,2:T(2,128)(2,1)S(1)}, bf16[1,2,1,256,512]{3,1,4,0,2:T(2,128)(2,1)S(1)}, u32[]{:S(2)}, u32[]{:S(2)}) collective-permute-start(bf16[1,2,1,256,512]{3,1,4,0,2:T(2,128)(2,1)S(1)} %get-tuple-element.119), channel_id=1, source_target_pairs={{0,12},{2,14},{4,0},{6,2},{8,4},{10,6},{12,8},{14,10},{1,13},{3,15... | collective-permute-start | bytes 1572872 | tf_op jit(solution)/shard_map/ppermute | solution.py:36
  559.1 26.8 %collective-permute-start.10 = (bf16[1,2,1,256,512]{3,1,4,0,2:T(2,128)(2,1)S(1)}, bf16[1,2,1,256,512]{3,1,4,0,2:T(2,128)(2,1)S(1)}, u32[]{:S(2)}, u32[]{:S(2)}) collective-permute-start(bf16[1,2,1,256,512]{3,1,4,0,2:T(2,128)(2,1)S(1)} %get-tuple-element.118), channel_id=1, source_target_pairs={{0,14},{2,0},{4,2},{6,4},{8,6},{10,8},{12,10},{14,12},{1,15},{3,1}... | collective-permute-start | bytes 1572872 | tf_op jit(solution)/shard_map/ppermute | solution.py:36
  601.6 19.8 %copy.63 = bf16[2,2,128,256,4,4]{2,1,5,4,3,0:T(2,128)(2,1)} copy(bf16[2,2,128,256,4,4]{3,0,5,2,4,1:T(2,128)(2,1)} %bitcast.176) | data formatting | bytes 8388608 | tf_op jit(solution)/shard_map/transpose | solution.py:141
  629.0 7.8 copy.64
  639.7 23.7 %all-gather.2.cloned.1.call-done = bf16[2,2,256,32,128]{4,3,2,0,1:T(8,128)(2,1)} async-done(((bf16[2,1,256,32,128]{4,3,2,0,1:T(8,128)(2,1)}), bf16[2,2,256,32,128]{4,3,2,0,1:T(8,128)(2,1)}) %all-gather.2.cloned.1.call-update) | async-done | bytes 8388624 | tf_op jit(solution)/shard_map/all_gather | solution.py:144
  663.4 8.4 copy.65
  671.8 11.5 %broadcast_in_dim.13 = f32[8,32,2,2,64,128]{5,4,3,2,1,0:T(8,128)} broadcast(f32[]{:T(128)} %constant.207.clone.1), dimensions={} | broadcast | bytes 33554436 | tf_op jit(solution)/shard_map/broadcast_in_dim | solution.py:151
  683.3 366.9 %while.11 = (s32[]{:T(128)}, f32[8,32,2,2,64,128]{5,4,3,2,1,0:T(8,128)}, s32[]{:T(128)}, s32[8]{0:T(128)S(1)}, s32[14,64]{1,0:T(8,128)}, /*index=5*/bf16[2,2,256...) while((s32[]{:T(128)}, ...), condition=%wide.region_6.8_spmd, body=%wide.region_4.7_spmd.sunk | while | flops 563612416 | bytes 78656224 | solution.py:161
  712.9 8.8 mul.778
  758.7 8.8 mul.778
  804.5 8.8 mul.778
  850.2 8.8 mul.778
  896.0 8.8 mul.778
  941.7 8.8 mul.778
  987.5 8.8 mul.778
  1033.3 8.8 mul.778
  (246 shorter events, 426.5 us)
Async XLA Ops:
  6.5 295.6 %copy-start.7 = (f32[16,2048]{1,0:T(8,128)S(1)}, f32[16,2048]{1,0:T(8,128)}, u32[]{:S(2)}) copy-start(f32[16,2048]{1,0:T(8,128)} %param.13) | copy-start | bytes 393220
  6.5 656.8 %all-gather.2.cloned.1.call-start = ((), (), s32[]{:S(2)}) async-start(), calls=%async_computation | async-start | bytes 12582912 | tf_op jit(solution)/shard_map/all_gather | solution.py:144
  12.9 95.1 %collective-permute-start = (bf16[2,128,4,2048]{1,3,2,0:T(8,128)(2,1)}, bf16[2,128,4,2048]{1,3,2,0:T(8,128)(2,1)S(1)}, u32[]{:S(2)}, u32[]{:S(2)}) collective-permute-start(bf16[2,128,4,2048]{1,3,2,0:T(8,128)(2,1)} %bitcast.179), channel_id=1, source_target_pairs={{0,2},{2,4},{4,6},{1,3},{3,5},{5,7},{8,10},{10,12},{12,14},{9,11},... | collective-permute-start | bytes 12582920 | tf_op jit(solution)/shard_map/ppermute | solution.py:48
  108.0 187.6 %copy-start.6 = (bf16[2,128,4,2048]{1,3,2,0:T(8,128)(2,1)}, bf16[2,128,4,2048]{1,3,2,0:T(8,128)(2,1)S(1)}, u32[]{:S(2)}) copy-start(bf16[2,128,4,2048]{1,3,2,0:T(8,128)(2,1)S(1)} %collective-permute-done) | copy-start | bytes 12582916
  108.0 93.2 %collective-permute-start.1 = (bf16[2,128,4,2048]{1,3,2,0:T(8,128)(2,1)S(1)}, bf16[2,128,4,2048]{1,3,2,0:T(8,128)(2,1)S(1)}, u32[]{:S(2)}, u32[]{:S(2)}) collective-permute-start(bf16[2,128,4,2048]{1,3,2,0:T(8,128)(2,1)S(1)} %collective-permute-done), channel_id=1, source_target_pairs={{0,2},{2,4},{4,6},{1,3},{3,5},{5,7},{8,10},{10,12},{12,14},{9,11},... | collective-permute-start | bytes 12582920 | tf_op jit(solution)/shard_map/ppermute | solution.py:48
  201.2 1.9 copy-start.4
  203.1 92.4 %collective-permute-start.2 = (bf16[2,128,4,2048]{1,3,2,0:T(8,128)(2,1)S(1)}, bf16[2,128,4,2048]{1,3,2,0:T(8,128)(2,1)}, u32[]{:S(2)}, u32[]{:S(2)}) collective-permute-start(bf16[2,128,4,2048]{1,3,2,0:T(8,128)(2,1)S(1)} %collective-permute-done.1), channel_id=1, source_target_pairs={{0,2},{2,4},{4,6},{1,3},{3,5},{5,7},{8,10},{10,12},{12,14},{9,11},... | collective-permute-start | bytes 12582920 | tf_op jit(solution)/shard_map/ppermute | solution.py:48
  295.5 91.9 %collective-permute-start.3 = (bf16[2,128,4,2048]{1,3,2,0:T(8,128)(2,1)}, bf16[2,128,4,2048]{1,3,2,0:T(8,128)(2,1)}, u32[]{:S(2)}, u32[]{:S(2)}) collective-permute-start(bf16[2,128,4,2048]{1,3,2,0:T(8,128)(2,1)} %collective-permute-done.2), channel_id=1, source_target_pairs={{0,2},{2,4},{4,6},{1,3},{3,5},{5,7},{8,10},{10,12},{12,14},{9,11},... | collective-permute-start | bytes 12582920 | tf_op jit(solution)/shard_map/ppermute | solution.py:48
  389.9 7.1 copy-start.5
  393.6 3.4 copy-start.2
  398.4 5.8 copy-start
  404.2 3.2 copy-start.1
  514.8 18.7 %collective-permute-start.4 = (bf16[1,2,1,256,512]{3,1,4,0,2:T(2,128)(2,1)}, bf16[1,2,1,256,512]{3,1,4,0,2:T(2,128)(2,1)}, u32[]{:S(2)}, u32[]{:S(2)}) collective-permute-start(bf16[1,2,1,256,512]{3,1,4,0,2:T(2,128)(2,1)} %get-tuple-element.124), channel_id=1, source_target_pairs={{0,2},{2,4},{4,6},{6,8},{8,10},{10,12},{12,14},{14,0},{1,3},{3,5},... | collective-permute-start | bytes 1572872 | tf_op jit(solution)/shard_map/ppermute | solution.py:36
  517.3 41.8 %collective-permute-start.5 = (bf16[1,2,1,256,512]{3,1,4,0,2:T(2,128)(2,1)S(1)}, bf16[1,2,1,256,512]{3,1,4,0,2:T(2,128)(2,1)}, u32[]{:S(2)}, u32[]{:S(2)}) collective-permute-start(bf16[1,2,1,256,512]{3,1,4,0,2:T(2,128)(2,1)S(1)} %get-tuple-element.123), channel_id=1, source_target_pairs={{0,4},{2,6},{4,8},{6,10},{8,12},{10,14},{12,0},{14,2},{1,5},{3,7},... | collective-permute-start | bytes 1572872 | tf_op jit(solution)/shard_map/ppermute | solution.py:36
  520.1 68.0 %collective-permute-start.6 = (bf16[1,2,1,256,512]{3,1,4,0,2:T(2,128)(2,1)S(1)}, bf16[1,2,1,256,512]{3,1,4,0,2:T(2,128)(2,1)}, u32[]{:S(2)}, u32[]{:S(2)}) collective-permute-start(bf16[1,2,1,256,512]{3,1,4,0,2:T(2,128)(2,1)S(1)} %get-tuple-element.122), channel_id=1, source_target_pairs={{0,6},{2,8},{4,10},{6,12},{8,14},{10,0},{12,2},{14,4},{1,7},{3,9},... | collective-permute-start | bytes 1572872 | tf_op jit(solution)/shard_map/ppermute | solution.py:36
  522.4 67.9 %collective-permute-start.7 = (bf16[1,2,1,256,512]{3,1,4,0,2:T(2,128)(2,1)S(1)}, bf16[1,2,1,256,512]{3,1,4,0,2:T(2,128)(2,1)}, u32[]{:S(2)}, u32[]{:S(2)}) collective-permute-start(bf16[1,2,1,256,512]{3,1,4,0,2:T(2,128)(2,1)S(1)} %get-tuple-element.121), channel_id=1, source_target_pairs={{0,8},{2,10},{4,12},{6,14},{8,0},{10,2},{12,4},{14,6},{1,9},{3,11}... | collective-permute-start | bytes 1572872 | tf_op jit(solution)/shard_map/ppermute | solution.py:36
  522.9 69.6 %collective-permute-start.8 = (bf16[1,2,1,256,512]{3,1,4,0,2:T(2,128)(2,1)S(1)}, bf16[1,2,1,256,512]{3,1,4,0,2:T(2,128)(2,1)}, u32[]{:S(2)}, u32[]{:S(2)}) collective-permute-start(bf16[1,2,1,256,512]{3,1,4,0,2:T(2,128)(2,1)S(1)} %get-tuple-element.120), channel_id=1, source_target_pairs={{0,10},{2,12},{4,14},{6,0},{8,2},{10,4},{12,6},{14,8},{1,11},{3,13... | collective-permute-start | bytes 1572872 | tf_op jit(solution)/shard_map/ppermute | solution.py:36
  533.6 61.9 %collective-permute-start.9 = (bf16[1,2,1,256,512]{3,1,4,0,2:T(2,128)(2,1)S(1)}, bf16[1,2,1,256,512]{3,1,4,0,2:T(2,128)(2,1)S(1)}, u32[]{:S(2)}, u32[]{:S(2)}) collective-permute-start(bf16[1,2,1,256,512]{3,1,4,0,2:T(2,128)(2,1)S(1)} %get-tuple-element.119), channel_id=1, source_target_pairs={{0,12},{2,14},{4,0},{6,2},{8,4},{10,6},{12,8},{14,10},{1,13},{3,15... | collective-permute-start | bytes 1572872 | tf_op jit(solution)/shard_map/ppermute | solution.py:36
  559.1 41.3 %collective-permute-start.10 = (bf16[1,2,1,256,512]{3,1,4,0,2:T(2,128)(2,1)S(1)}, bf16[1,2,1,256,512]{3,1,4,0,2:T(2,128)(2,1)S(1)}, u32[]{:S(2)}, u32[]{:S(2)}) collective-permute-start(bf16[1,2,1,256,512]{3,1,4,0,2:T(2,128)(2,1)S(1)} %get-tuple-element.118), channel_id=1, source_target_pairs={{0,14},{2,0},{4,2},{6,4},{8,6},{10,8},{12,10},{14,12},{1,15},{3,1}... | collective-permute-start | bytes 1572872 | tf_op jit(solution)/shard_map/ppermute | solution.py:36
  671.8 11.5 %copy-start.9 = (s32[6]{0:T(128)S(1)}, s32[6]{0:T(128)}, u32[]{:S(2)}) copy-start(s32[6]{0:T(128)} %constant.202.clone.1) | copy-start | bytes 76
  702.5 1.2 copy-start.3
  748.3 1.2 copy-start.3
  885.5 1.2 copy-start.3
  1022.8 1.2 copy-start.3
  (5 other events, 5.6 us)
Sparse Core Ops, SparseCore 0:
  637.0 26.3 all-gather.1
